TPU v7x, 32 devices: a whole 2x2x4 slice. The times are simulated.
32 devices in a mesh: groups: 2 (over x), rows: 16 (over z, y, core).
Axes of the slice: x: 2, y: 2, z: 4, core: 2. Of those that a mesh axis runs over, the one named last changes fastest.
Arguments:
- features: bfloat16 [512, 256, 128], P('rows', 'groups'), parts along dimension 1, may hold values from -6 to 6
- weights: bfloat16 [1, 512, 8, 128, 128], P(None, 'rows'), may hold values from -0.25 to 0.25
- biases: float32 [1, 512, 128], P(None, 'rows'), may hold values from -3 to 3
- dest_dev: int32 [1, 512, 8], replicated, may hold values from 0 to 15, all different within a row; in each aligned block of 32 rows (0 to 31, 32 to 63, ..., all dimensions but the last counted through in order) at most 32 rows name the same one
- dest_local: int32 [1, 512, 8], replicated, may hold values from 0 to 31
Outputs:
- outputs: bfloat16 [512, 256, 128], P('rows', 'groups'), parts along dimension 1
There are 2 independent parts, one for each index of `groups`. A program takes and returns all parts, laid end to end along the dimension named above; an argument that names none is the same for every part. Nothing has to cross between parts.
Inputs may be any that keep to these rules, and one draw needn't show every extreme that they name: `dest_dev`: the 8 entries of one input block name different owners; in one layer, the 32 input blocks of one owner name any one owner at most 32 times, and in some layers some owner is named exactly 32 times by one owner's blocks.
All inputs are finite; a program needn't handle non-finite values.
Results may differ from a plain program's by a relative error of at most 0.001.
Values sent between devices are 32-bit elements; how exact they have to be, the bound alone decides.
A program may use at most 320 MiB of HBM per device.

v0:
```python
import functools

import jax
import jax.numpy as jnp
from jax import lax
from jax.experimental import pallas as pl
from jax.experimental.pallas import tpu as pltpu
from jax.sharding import PartitionSpec as P

MIB = 1024 * 1024


def partial_kernel(pos_ref, feat_ref, weight_ref, out_ref, acc, sem):
    step = pl.program_id(0)
    per_step, degree = weight_ref.shape[:2]
    owners, owned = acc.shape[:2]

    @pl.when(step == 0)
    def _():
        @pl.loop(0, owners)
        def _(o):
            @pl.loop(0, owned)
            def _(b):
                acc[o, b] = jnp.zeros(acc.shape[2:], acc.dtype)

    @pl.loop(0, per_step)
    def _(i):
        block = feat_ref[i]
        products = [
            jnp.dot(block, weight_ref[i, k], preferred_element_type=jnp.float32)
            for k in range(degree)
        ]
        base = (step * per_step + i) * degree
        for k in range(degree):
            position = pos_ref[base + k]
            acc[position // owned, position % owned] += products[k]

    @pl.when(step == pl.num_programs(0) - 1)
    def _():
        copy = pltpu.make_async_copy(acc, out_ref, sem)
        copy.start()
        copy.wait()


def local_partials(position, features, weights, owners, owned):
    count, samples, width = features.shape
    degree = weights.shape[1]
    per_step = min(4, count)
    return pl.pallas_call(
        partial_kernel,
        out_shape=jax.ShapeDtypeStruct((owners, owned, samples, width), jnp.float32),
        grid_spec=pltpu.PrefetchScalarGridSpec(
            num_scalar_prefetch=1,
            grid=(count // per_step,),
            in_specs=[
                pl.BlockSpec((per_step, samples, width), lambda s, pos: (s, 0, 0)),
                pl.BlockSpec((per_step, degree, width, width), lambda s, pos: (s, 0, 0, 0)),
            ],
            out_specs=pl.BlockSpec(memory_space=pl.ANY),
            scratch_shapes=[
                pltpu.VMEM((owners, owned, samples, width), jnp.float32),
                pltpu.SemaphoreType.DMA,
            ],
        ),
        compiler_params=pltpu.CompilerParams(
            dimension_semantics=("arbitrary",), vmem_limit_bytes=48 * MIB
        ),
    )(position, features, weights)


def farthest_first(z, nz):
    near = jnp.minimum(z, nz - 1 - z)
    far = nz - 1 - near
    sign = jnp.where(2 * z < nz, 1, -1)
    places = []
    for t in range(nz):
        u = t - (far - near)
        alone = z + sign * (far - t)
        paired = jnp.where(u % 2 == 0, z + sign * (near - u // 2), z - sign * (near - u // 2))
        places.append(jnp.where(u < 0, alone, paired))
    return places


def scatter_kernel(nz, ny, p_ref, bias_ref, out_ref, held, own, from_y, from_low, from_high,
                   own_sem, c_send, c_recv, y_send, y_recv, up_send, up_recv, down_send, down_recv):
    rank = lax.axis_index("rows")
    c = rank % 2
    y = (rank // 2) % ny
    z = rank // (2 * ny)
    owned = out_ref.shape[0]

    def row(z_at, y_at, c_at):
        return (z_at * ny + y_at) * 2 + c_at

    def remote(src, dst, send, recv, target):
        return pltpu.make_async_remote_copy(
            src_ref=src, dst_ref=dst, send_sem=send, recv_sem=recv,
            device_id={"rows": target}, device_id_type=pl.DeviceIdType.MESH,
        )

    sibling = row(z, y, 1 - c)
    peer = row(z, ny - 1 - y, c)
    above = row(z + 1, y, c)
    below = row(z - 1, y, c)
    has_above, has_below = z < nz - 1, z > 0

    barrier = pltpu.get_barrier_semaphore()

    def greet(target):
        pl.semaphore_signal(
            barrier, inc=1, device_id={"rows": target}, device_id_type=pl.DeviceIdType.MESH
        )

    greet(sibling)
    if ny > 1:
        greet(peer)
    pl.when(has_above)(lambda: greet(above))
    pl.when(has_below)(lambda: greet(below))
    pl.semaphore_wait(barrier, ny + jnp.where(has_above, 1, 0) + jnp.where(has_below, 1, 0))

    def add(dst, srcs):
        @pl.loop(0, owned)
        def _(b):
            total = dst[b]
            for src in srcs:
                total = total + src[b]
            dst[b] = total

    order = farthest_first(z, nz)

    def y_of(h):
        return y if h == ny - 1 else ny - 1 - y

    pieces = [(h, place) for place in order for h in range(ny)]

    def to_sibling(h, place):
        return remote(p_ref.at[row(place, y_of(h), 1 - c)], held.at[h, place],
                      c_send.at[h, place], c_recv.at[h, place], sibling)

    def load(n):
        h, place = pieces[n]
        return pltpu.make_async_copy(
            p_ref.at[row(place, y_of(h), c)], own.at[n % 2], own_sem.at[n % 2]
        )

    def to_peer(place):
        return remote(held.at[0, place], from_y.at[place], y_send.at[place], y_recv.at[place], peer)

    def to_above(place):
        return remote(held.at[ny - 1, place], from_low.at[place - 1],
                      up_send.at[place - 1], up_recv.at[place - 1], above)

    def to_below(place):
        return remote(held.at[ny - 1, place], from_high.at[place],
                      down_send.at[place], down_recv.at[place], below)

    load(0).start()
    for h, place in pieces:
        to_sibling(h, place).start()
    for n, (h, place) in enumerate(pieces):
        if n + 1 < len(pieces):
            load(n + 1).start()
        load(n).wait()
        to_sibling(h, place).wait_recv()
        add(held.at[h, place], [own.at[n % 2]])
        if h < ny - 1:
            to_peer(place).start()

    for t, place in enumerate(order[:-1]):
        if ny > 1:
            to_peer(place).wait_recv()
            add(held.at[ny - 1, place], [from_y.at[place]])

        @pl.when(place > z)
        def _():
            @pl.when(has_below)
            def _():
                to_above(place).wait_recv()
                add(held.at[ny - 1, place], [from_low.at[place - 1]])
            to_above(place).start()

        @pl.when(place < z)
        def _():
            @pl.when(has_above)
            def _():
                to_below(place).wait_recv()
                add(held.at[ny - 1, place], [from_high.at[place]])
            to_below(place).start()

    if ny > 1:
        to_peer(z).wait_recv()
        add(held.at[ny - 1, z], [from_y.at[z]])

    @pl.when(has_below)
    def _():
        to_above(z).wait_recv()
        add(held.at[ny - 1, z], [from_low.at[z - 1]])

    @pl.when(has_above)
    def _():
        to_below(z).wait_recv()
        add(held.at[ny - 1, z], [from_high.at[z]])

    @pl.loop(0, owned)
    def _(b):
        total = held[ny - 1, z, b] + bias_ref[b]
        out_ref[b] = jnp.maximum(total, 0.0).astype(out_ref.dtype)

    for h, place in pieces:
        to_sibling(h, place).wait_send()
    for place in order:
        if ny > 1:
            to_peer(place).wait_send()
        pl.when(place > z)(lambda place=place: to_above(place).wait_send())
        pl.when(place < z)(lambda place=place: to_below(place).wait_send())


def scatter_sum(partials, bias, nz, ny):
    owners, owned, samples, width = partials.shape
    chunk = (owned, samples, width)
    dma = pltpu.SemaphoreType.DMA
    vmem = pl.BlockSpec(memory_space=pltpu.VMEM)
    return pl.pallas_call(
        functools.partial(scatter_kernel, nz, ny),
        out_shape=jax.ShapeDtypeStruct(chunk, jnp.bfloat16),
        in_specs=[pl.BlockSpec(memory_space=pl.ANY), vmem],
        out_specs=vmem,
        scratch_shapes=[
            pltpu.VMEM((ny, nz) + chunk, jnp.float32),
            pltpu.VMEM((2,) + chunk, jnp.float32),
            pltpu.VMEM((nz if ny > 1 else 1,) + chunk, jnp.float32),
            pltpu.VMEM((nz - 1,) + chunk, jnp.float32),
            pltpu.VMEM((nz - 1,) + chunk, jnp.float32),
            dma((2,)),
            dma((ny, nz)), dma((ny, nz)),
            dma((nz,)), dma((nz,)),
            dma((nz,)), dma((nz,)),
            dma((nz,)), dma((nz,)),
        ],
        compiler_params=pltpu.CompilerParams(
            collective_id=0, has_side_effects=True, vmem_limit_bytes=56 * MIB
        ),
    )(partials, bias[:, None, :])


def shards(ny, features, weights, biases, dest_dev, dest_local):
    owners = lax.axis_size("rows")
    rank = lax.axis_index("rows")
    owned = features.shape[0]
    position = dest_dev[0] * owned + dest_local[0]
    position = lax.dynamic_slice_in_dim(position, rank * owned, owned, 0).reshape(-1)
    partials = local_partials(position, features, weights[0], owners, owned)
    return scatter_sum(partials, biases[0], owners // (2 * ny), ny)


def solution(mesh):
    ny = 4 // mesh.shape["groups"]
    in_specs = (
        P("rows", "groups", None),
        P(None, "rows", None, None, None),
        P(None, "rows", None),
        P(),
        P(),
    )
    return jax.shard_map(
        functools.partial(shards, ny), mesh=mesh, in_specs=in_specs,
        out_specs=P("rows", "groups", None), check_vma=False,
    )
```

profile of v0, /device:TPU:0, one launch (start us, length us, event | category | flops | bytes accessed | tf_op | source)
XLA Modules:
  0.0 227.1 jit_solution(15818458957273559114)
XLA Ops:
  0.0 0.8 dynamic-slice_add_fusion
  0.8 0.1 copy.6
  0.9 0.1 reshape.8.pos_ref
  0.9 0.0 copy-start
  1.0 1.2 copy-done
  2.2 24.6 %shard_map.55.p_ref = f32[16,32,128,128]{3,2,1,0:T(8,128)} custom-call(s32[256]{0:T(256)S(1)} %reshape.8.pos_ref, bf16[32,128,128]{2,1,0:T(8,128)(2,1)S(1)} %copy-done, bf16[32,8,128,128]{3,2,1,0:T(8,128)(2,1)} %bitcast.2), custom_call_target="tpu_custom_call" | custom-call | tf_op jit(solution)/shard_map/pallas_call | solution.py:49
  26.8 198.0 %shard_map.56 = bf16[32,128,128]{2,1,0:T(8,128)(2,1)} custom-call(f32[16,32,128,128]{3,2,1,0:T(8,128)} %shard_map.55.p_ref, f32[32,1,128]{2,1,0:T(1,128)} %bitcast.3), custom_call_target="tpu_custom_call" | custom-call | tf_op jit(solution)/shard_map/pallas_call | solution.py:223
  224.8 2.3 %copy.8 = bf16[32,128,128]{2,1,0:T(8,128)(2,1)} copy(bf16[32,128,128]{2,1,0:T(8,128)(2,1)} %shard_map.56) | data formatting | bytes 2097152
Async XLA Ops:
  0.9 1.2 copy-start
where the time goes:
time: 228 us; the launch traced here: 227 us
  Pallas kernels  223 us (98%)
  local copies, waits for them, and re-layouts  3.7 us (2%)
    pallas_call x1, Pallas kernels, scatter_sum(): pl.pallas_call(functools.partial(scatter_kernel, nz, ny), out_shape=jax.S...  198 us
    pallas_call x1, Pallas kernels, local_partials(): pl.pallas_call(partial_kernel, out_shape=jax.ShapeDtypeStruct((owners, ow...  24.6 us

commit v1 on v0

--- a/solution.py
+++ b/solution.py
@@ -81,8 +81,10 @@
     return places
 
 
-def scatter_kernel(nz, ny, p_ref, bias_ref, out_ref, held, own, from_y, from_low, from_high,
-                   own_sem, c_send, c_recv, y_send, y_recv, up_send, up_recv, down_send, down_recv):
+def scatter_kernel(nz, ny, lead, p_ref, bias_ref, out_ref, held, own, from_y, from_low, from_high,
+                   lead_y, lead_low, lead_high,
+                   own_sem, c_send, c_recv, y_send, y_recv, up_send, up_recv, down_send, down_recv,
+                   ly_send, ly_recv, lup_send, lup_recv, ldown_send, ldown_recv):
     rank = lax.axis_index("rows")
     c = rank % 2
     y = (rank // 2) % ny
@@ -118,13 +120,13 @@
     pl.when(has_below)(lambda: greet(below))
     pl.semaphore_wait(barrier, ny + jnp.where(has_above, 1, 0) + jnp.where(has_below, 1, 0))
 
-    def add(dst, srcs):
-        @pl.loop(0, owned)
+    def add(dst, src, start=0):
+        @pl.loop(0, src.shape[0])
         def _(b):
-            total = dst[b]
-            for src in srcs:
-                total = total + src[b]
-            dst[b] = total
+            dst[b + start] += src[b]
+
+    rest = pl.ds(lead, owned - lead)
+    first = pl.ds(0, max(lead, 1))
 
     order = farthest_first(z, nz)
 
@@ -144,15 +146,30 @@
         )
 
     def to_peer(place):
-        return remote(held.at[0, place], from_y.at[place], y_send.at[place], y_recv.at[place], peer)
+        return remote(held.at[0, place, rest], from_y.at[place], y_send.at[place], y_recv.at[place], peer)
 
     def to_above(place):
-        return remote(held.at[ny - 1, place], from_low.at[place - 1],
+        return remote(held.at[ny - 1, place, rest], from_low.at[place - 1],
                       up_send.at[place - 1], up_recv.at[place - 1], above)
 
     def to_below(place):
-        return remote(held.at[ny - 1, place], from_high.at[place],
+        return remote(held.at[ny - 1, place, rest], from_high.at[place],
                       down_send.at[place], down_recv.at[place], below)
+
+    def lead_above(place):
+        return remote(held.at[:, place, first], lead_low.at[place - 1],
+                      lup_send.at[place - 1], lup_recv.at[place - 1], above)
+
+    def lead_below(place):
+        return remote(held.at[:, place, first], lead_high.at[place],
+                      ldown_send.at[place], ldown_recv.at[place], below)
+
+    def lead_peer():
+        return remote(held.at[0, z, first], lead_y, ly_send, ly_recv, peer)
+
+    def add_lead(place, src):
+        for h in range(ny):
+            add(held.at[h, place], src.at[h])
 
     load(0).start()
     for h, place in pieces:
@@ -162,21 +179,38 @@
             load(n + 1).start()
         load(n).wait()
         to_sibling(h, place).wait_recv()
-        add(held.at[h, place], [own.at[n % 2]])
+        add(held.at[h, place], own.at[n % 2])
         if h < ny - 1:
             to_peer(place).start()
+        elif lead:
+            pl.when((place > z) & (z == 0))(lambda: lead_above(place).start())
+            pl.when((place < z) & (z == nz - 1))(lambda: lead_below(place).start())
+
+    if lead:
+        for place in order[:-1]:
+            @pl.when((place > z) & has_below)
+            def _():
+                lead_above(place).wait_recv()
+                add_lead(place, lead_low.at[place - 1])
+                lead_above(place).start()
+
+            @pl.when((place < z) & has_above)
+            def _():
+                lead_below(place).wait_recv()
+                add_lead(place, lead_high.at[place])
+                lead_below(place).start()
 
     for t, place in enumerate(order[:-1]):
         if ny > 1:
             to_peer(place).wait_recv()
-            add(held.at[ny - 1, place], [from_y.at[place]])
+            add(held.at[ny - 1, place], from_y.at[place], lead)
 
         @pl.when(place > z)
         def _():
             @pl.when(has_below)
             def _():
                 to_above(place).wait_recv()
-                add(held.at[ny - 1, place], [from_low.at[place - 1]])
+                add(held.at[ny - 1, place], from_low.at[place - 1], lead)
             to_above(place).start()
 
         @pl.when(place < z)
@@ -184,22 +218,37 @@
             @pl.when(has_above)
             def _():
                 to_below(place).wait_recv()
-                add(held.at[ny - 1, place], [from_high.at[place]])
+                add(held.at[ny - 1, place], from_high.at[place], lead)
             to_below(place).start()
+
+        if lead and t == 1:
+            @pl.when(has_below)
+            def _():
+                lead_above(z).wait_recv()
+                add_lead(z, lead_low.at[z - 1])
+
+            @pl.when(has_above)
+            def _():
+                lead_below(z).wait_recv()
+                add_lead(z, lead_high.at[z])
+            lead_peer().start()
 
     if ny > 1:
         to_peer(z).wait_recv()
-        add(held.at[ny - 1, z], [from_y.at[z]])
+        add(held.at[ny - 1, z], from_y.at[z], lead)
+    if lead:
+        lead_peer().wait_recv()
+        add(held.at[ny - 1, z], lead_y)
 
     @pl.when(has_below)
     def _():
         to_above(z).wait_recv()
-        add(held.at[ny - 1, z], [from_low.at[z - 1]])
+        add(held.at[ny - 1, z], from_low.at[z - 1], lead)
 
     @pl.when(has_above)
     def _():
         to_below(z).wait_recv()
-        add(held.at[ny - 1, z], [from_high.at[z]])
+        add(held.at[ny - 1, z], from_high.at[z], lead)
 
     @pl.loop(0, owned)
     def _(b):
@@ -213,27 +262,41 @@
             to_peer(place).wait_send()
         pl.when(place > z)(lambda place=place: to_above(place).wait_send())
         pl.when(place < z)(lambda place=place: to_below(place).wait_send())
+        if lead:
+            pl.when(place > z)(lambda place=place: lead_above(place).wait_send())
+            pl.when(place < z)(lambda place=place: lead_below(place).wait_send())
+    if lead:
+        lead_peer().wait_send()
 
 
 def scatter_sum(partials, bias, nz, ny):
     owners, owned, samples, width = partials.shape
     chunk = (owned, samples, width)
+    lead = owned * 5 // 32 if ny > 1 and nz > 2 else 0
+    rest = (owned - lead,) + chunk[1:]
+    first = (max(lead, 1),) + chunk[1:]
     dma = pltpu.SemaphoreType.DMA
     vmem = pl.BlockSpec(memory_space=pltpu.VMEM)
     return pl.pallas_call(
-        functools.partial(scatter_kernel, nz, ny),
+        functools.partial(scatter_kernel, nz, ny, lead),
         out_shape=jax.ShapeDtypeStruct(chunk, jnp.bfloat16),
         in_specs=[pl.BlockSpec(memory_space=pl.ANY), vmem],
         out_specs=vmem,
         scratch_shapes=[
             pltpu.VMEM((ny, nz) + chunk, jnp.float32),
             pltpu.VMEM((2,) + chunk, jnp.float32),
-            pltpu.VMEM((nz if ny > 1 else 1,) + chunk, jnp.float32),
-            pltpu.VMEM((nz - 1,) + chunk, jnp.float32),
-            pltpu.VMEM((nz - 1,) + chunk, jnp.float32),
+            pltpu.VMEM((nz if ny > 1 else 1,) + rest, jnp.float32),
+            pltpu.VMEM((nz - 1,) + rest, jnp.float32),
+            pltpu.VMEM((nz - 1,) + rest, jnp.float32),
+            pltpu.VMEM(first, jnp.float32),
+            pltpu.VMEM((nz - 1, ny) + first if lead else (1, 1) + first, jnp.float32),
+            pltpu.VMEM((nz - 1, ny) + first if lead else (1, 1) + first, jnp.float32),
             dma((2,)),
             dma((ny, nz)), dma((ny, nz)),
             dma((nz,)), dma((nz,)),
+            dma((nz,)), dma((nz,)),
+            dma((nz,)), dma((nz,)),
+            dma, dma,
             dma((nz,)), dma((nz,)),
             dma((nz,)), dma((nz,)),
         ],

time: 228 us -> 207 us (0.908)
  Pallas kernels: 223 us -> 202 us
    pallas_call x1, Pallas kernels: 198 us -> 177 us  [scatter_sum(): pl.pallas_call(functools.partial(scatter_kernel, nz, ny, lead), out_shape...]
where the time goes in v1:
time: 207 us
  Pallas kernels  202 us (98%)
  local copies, waits for them, and re-layouts  3.7 us (2%)
    pallas_call x1, Pallas kernels, scatter_sum(): pl.pallas_call(functools.partial(scatter_kernel, nz, ny, lead), out_shape...  177 us
    pallas_call x1, Pallas kernels, local_partials(): pl.pallas_call(partial_kernel, out_shape=jax.ShapeDtypeStruct((owners, ow...  24.6 us

profile of v1, /device:TPU:0, one launch (start us, length us, event | category | flops | bytes accessed | tf_op | source)
XLA Modules:
  0.0 206.6 jit_solution(17032208018879771271)
XLA Ops:
  0.0 0.8 dynamic-slice_add_fusion
  0.8 0.1 copy.6
  0.9 0.1 reshape.8.pos_ref
  0.9 0.0 copy-start
  1.0 1.2 copy-done
  2.2 24.6 %shard_map.55.p_ref = f32[16,32,128,128]{3,2,1,0:T(8,128)} custom-call(s32[256]{0:T(256)S(1)} %reshape.8.pos_ref, bf16[32,128,128]{2,1,0:T(8,128)(2,1)S(1)} %copy-done, bf16[32,8,128,128]{3,2,1,0:T(8,128)(2,1)} %bitcast.2), custom_call_target="tpu_custom_call" | custom-call | tf_op jit(solution)/shard_map/pallas_call | solution.py:49
  26.8 177.4 %shard_map.56 = bf16[32,128,128]{2,1,0:T(8,128)(2,1)} custom-call(f32[16,32,128,128]{3,2,1,0:T(8,128)} %shard_map.55.p_ref, f32[32,1,128]{2,1,0:T(1,128)} %bitcast.3), custom_call_target="tpu_custom_call" | custom-call | tf_op jit(solution)/shard_map/pallas_call | solution.py:280
  204.3 2.3 %copy.8 = bf16[32,128,128]{2,1,0:T(8,128)(2,1)} copy(bf16[32,128,128]{2,1,0:T(8,128)(2,1)} %shard_map.56) | data formatting | bytes 2097152
Async XLA Ops:
  0.9 1.2 copy-start

commit v2 on v1

--- a/solution.py
+++ b/solution.py
@@ -10,62 +10,20 @@
 MIB = 1024 * 1024
 
 
-def partial_kernel(pos_ref, feat_ref, weight_ref, out_ref, acc, sem):
-    step = pl.program_id(0)
-    per_step, degree = weight_ref.shape[:2]
-    owners, owned = acc.shape[:2]
-
-    @pl.when(step == 0)
-    def _():
-        @pl.loop(0, owners)
-        def _(o):
-            @pl.loop(0, owned)
-            def _(b):
-                acc[o, b] = jnp.zeros(acc.shape[2:], acc.dtype)
-
-    @pl.loop(0, per_step)
-    def _(i):
-        block = feat_ref[i]
-        products = [
-            jnp.dot(block, weight_ref[i, k], preferred_element_type=jnp.float32)
-            for k in range(degree)
-        ]
-        base = (step * per_step + i) * degree
-        for k in range(degree):
-            position = pos_ref[base + k]
-            acc[position // owned, position % owned] += products[k]
-
-    @pl.when(step == pl.num_programs(0) - 1)
-    def _():
-        copy = pltpu.make_async_copy(acc, out_ref, sem)
-        copy.start()
-        copy.wait()
-
-
-def local_partials(position, features, weights, owners, owned):
-    count, samples, width = features.shape
-    degree = weights.shape[1]
-    per_step = min(4, count)
-    return pl.pallas_call(
-        partial_kernel,
-        out_shape=jax.ShapeDtypeStruct((owners, owned, samples, width), jnp.float32),
-        grid_spec=pltpu.PrefetchScalarGridSpec(
-            num_scalar_prefetch=1,
-            grid=(count // per_step,),
-            in_specs=[
-                pl.BlockSpec((per_step, samples, width), lambda s, pos: (s, 0, 0)),
-                pl.BlockSpec((per_step, degree, width, width), lambda s, pos: (s, 0, 0, 0)),
-            ],
-            out_specs=pl.BlockSpec(memory_space=pl.ANY),
-            scratch_shapes=[
-                pltpu.VMEM((owners, owned, samples, width), jnp.float32),
-                pltpu.SemaphoreType.DMA,
-            ],
-        ),
-        compiler_params=pltpu.CompilerParams(
-            dimension_semantics=("arbitrary",), vmem_limit_bytes=48 * MIB
-        ),
-    )(position, features, weights)
+def chunk_tables(dests, locals_, owners):
+    owned, degree = dests.shape
+    own = jnp.arange(owned, dtype=jnp.int32)
+    named = dests[None] == jnp.arange(owners, dtype=jnp.int32)[:, None, None]
+    entry = jnp.max(jnp.where(named, jnp.arange(degree, dtype=jnp.int32), 0), axis=2)
+    entry = entry + own * degree
+    block = jnp.max(jnp.where(named, locals_[None], -1), axis=2)
+    same = (block[:, :, None] == block[:, None, :]) & (block[:, None, :] >= 0)
+    earlier = same & (own[None, None, :] < own[None, :, None])
+    before = jnp.max(jnp.where(earlier, own, -1), axis=2)
+    last = jnp.max(jnp.where(block[:, None, :] == own[None, :, None], own, -1), axis=2)
+    before = jnp.where(before < 0, owned, before)
+    last = jnp.where(last < 0, owned, last)
+    return jnp.stack([entry, before, last])
 
 
 def farthest_first(z, nz):
@@ -81,9 +39,10 @@
     return places
 
 
-def scatter_kernel(nz, ny, lead, p_ref, bias_ref, out_ref, held, own, from_y, from_low, from_high,
+def scatter_kernel(nz, ny, lead, table_ref, feat_ref, weight_hbm, bias_ref, out_ref,
+                   weight_ref, held, sums, staged, from_y, from_low, from_high,
                    lead_y, lead_low, lead_high,
-                   own_sem, c_send, c_recv, y_send, y_recv, up_send, up_recv, down_send, down_recv,
+                   weight_sem, c_send, c_recv, y_send, y_recv, up_send, up_recv, down_send, down_recv,
                    ly_send, ly_recv, lup_send, lup_recv, ldown_send, ldown_recv):
     rank = lax.axis_index("rows")
     c = rank % 2
@@ -106,6 +65,8 @@
     below = row(z - 1, y, c)
     has_above, has_below = z < nz - 1, z > 0
 
+    load_weights = pltpu.make_async_copy(weight_hbm, weight_ref, weight_sem)
+    load_weights.start()
     barrier = pltpu.get_barrier_semaphore()
 
     def greet(target):
@@ -135,15 +96,18 @@
 
     pieces = [(h, place) for place in order for h in range(ny)]
 
-    def to_sibling(h, place):
-        return remote(p_ref.at[row(place, y_of(h), 1 - c)], held.at[h, place],
+    def to_sibling(n):
+        h, place = pieces[n]
+        return remote(staged.at[n % 2], held.at[h, place],
                       c_send.at[h, place], c_recv.at[h, place], sibling)
 
-    def load(n):
-        h, place = pieces[n]
-        return pltpu.make_async_copy(
-            p_ref.at[row(place, y_of(h), c)], own.at[n % 2], own_sem.at[n % 2]
-        )
+    def add_products(owner):
+        @pl.loop(0, owned, unroll=min(8, owned))
+        def _(i):
+            product = jnp.dot(
+                feat_ref[i], weight_ref[table_ref[0, owner, i]], preferred_element_type=jnp.float32
+            )
+            sums[i] = product + sums[table_ref[1, owner, i]]
 
     def to_peer(place):
         return remote(held.at[0, place, rest], from_y.at[place], y_send.at[place], y_recv.at[place], peer)
@@ -171,15 +135,26 @@
         for h in range(ny):
             add(held.at[h, place], src.at[h])
 
-    load(0).start()
-    for h, place in pieces:
-        to_sibling(h, place).start()
+    sums[owned] = jnp.zeros(sums.shape[1:], sums.dtype)
+    load_weights.wait()
     for n, (h, place) in enumerate(pieces):
-        if n + 1 < len(pieces):
-            load(n + 1).start()
-        load(n).wait()
-        to_sibling(h, place).wait_recv()
-        add(held.at[h, place], own.at[n % 2])
+        theirs, mine = row(place, y_of(h), 1 - c), row(place, y_of(h), c)
+        add_products(theirs)
+        if n >= 2:
+            to_sibling(n - 2).wait_send()
+
+        @pl.loop(0, owned)
+        def _(b):
+            staged[n % 2, b] = sums[table_ref[2, theirs, b]]
+
+        to_sibling(n).start()
+        add_products(mine)
+        to_sibling(n).wait_recv()
+
+        @pl.loop(0, owned)
+        def _(b):
+            held[h, place, b] += sums[table_ref[2, mine, b]]
+
         if h < ny - 1:
             to_peer(place).start()
         elif lead:
@@ -255,8 +230,8 @@
         total = held[ny - 1, z, b] + bias_ref[b]
         out_ref[b] = jnp.maximum(total, 0.0).astype(out_ref.dtype)
 
-    for h, place in pieces:
-        to_sibling(h, place).wait_send()
+    for n in range(max(0, len(pieces) - 2), len(pieces)):
+        to_sibling(n).wait_send()
     for place in order:
         if ny > 1:
             to_peer(place).wait_send()
@@ -269,8 +244,8 @@
         lead_peer().wait_send()
 
 
-def scatter_sum(partials, bias, nz, ny):
-    owners, owned, samples, width = partials.shape
+def scatter_sum(tables, features, weights, bias, nz, ny):
+    owned, samples, width = features.shape
     chunk = (owned, samples, width)
     lead = owned * 5 // 32 if ny > 1 and nz > 2 else 0
     rest = (owned - lead,) + chunk[1:]
@@ -280,10 +255,12 @@
     return pl.pallas_call(
         functools.partial(scatter_kernel, nz, ny, lead),
         out_shape=jax.ShapeDtypeStruct(chunk, jnp.bfloat16),
-        in_specs=[pl.BlockSpec(memory_space=pl.ANY), vmem],
+        in_specs=[pl.BlockSpec(memory_space=pltpu.SMEM), vmem, pl.BlockSpec(memory_space=pl.ANY), vmem],
         out_specs=vmem,
         scratch_shapes=[
+            pltpu.VMEM(weights.shape, weights.dtype),
             pltpu.VMEM((ny, nz) + chunk, jnp.float32),
+            pltpu.VMEM((owned + 1,) + chunk[1:], jnp.float32),
             pltpu.VMEM((2,) + chunk, jnp.float32),
             pltpu.VMEM((nz if ny > 1 else 1,) + rest, jnp.float32),
             pltpu.VMEM((nz - 1,) + rest, jnp.float32),
@@ -291,7 +268,7 @@
             pltpu.VMEM(first, jnp.float32),
             pltpu.VMEM((nz - 1, ny) + first if lead else (1, 1) + first, jnp.float32),
             pltpu.VMEM((nz - 1, ny) + first if lead else (1, 1) + first, jnp.float32),
-            dma((2,)),
+            dma,
             dma((ny, nz)), dma((ny, nz)),
             dma((nz,)), dma((nz,)),
             dma((nz,)), dma((nz,)),
@@ -301,19 +278,21 @@
             dma((nz,)), dma((nz,)),
         ],
         compiler_params=pltpu.CompilerParams(
-            collective_id=0, has_side_effects=True, vmem_limit_bytes=56 * MIB
+            collective_id=0, has_side_effects=True, vmem_limit_bytes=60 * MIB
         ),
-    )(partials, bias[:, None, :])
+    )(tables, features, weights, bias[:, None, :])
 
 
 def shards(ny, features, weights, biases, dest_dev, dest_local):
     owners = lax.axis_size("rows")
     rank = lax.axis_index("rows")
     owned = features.shape[0]
-    position = dest_dev[0] * owned + dest_local[0]
-    position = lax.dynamic_slice_in_dim(position, rank * owned, owned, 0).reshape(-1)
-    partials = local_partials(position, features, weights[0], owners, owned)
-    return scatter_sum(partials, biases[0], owners // (2 * ny), ny)
+    dests, locals_ = (
+        lax.dynamic_slice_in_dim(table[0], rank * owned, owned, 0) for table in (dest_dev, dest_local)
+    )
+    tables = chunk_tables(dests, locals_, owners)
+    blocks = weights.reshape((-1,) + weights.shape[3:])
+    return scatter_sum(tables, features, blocks, biases[0], owners // (2 * ny), ny)
 
 
 def solution(mesh):

time: 207 us -> 185 us (0.89)
  Pallas kernels: 202 us -> 180 us
    pallas_call x1 -> x0, Pallas kernels: 24.6 us -> none  [local_partials(): pl.pallas_call(partial_kernel, out_shape=jax.ShapeDtypeStruct((owners, ow...]
    pallas_call x1, Pallas kernels: 177 us -> 180 us  [scatter_sum(): pl.pallas_call(functools.partial(scatter_kernel, nz, ny, lead), out_shape...]
where the time goes in v2:
time: 185 us
  Pallas kernels  180 us (97%)
  local copies, waits for them, and re-layouts  3.09 us (2%)
    pallas_call x1, Pallas kernels, scatter_sum(): pl.pallas_call(functools.partial(scatter_kernel, nz, ny, lead), out_shape...  180 us

profile of v2, /device:TPU:0, one launch (start us, length us, event | category | flops | bytes accessed | tf_op | source)
XLA Modules:
  0.0 184.8 jit_solution(7876929625579380390)
XLA Ops:
  0.0 0.8 dynamic-slice_bitcast_fusion
  0.8 0.1 select_reduce_fusion.3
  0.9 0.7 select_reduce_fusion.1
  1.6 0.6 pad_add_fusion.table_ref
  2.3 180.2 %shard_map.55 = bf16[32,128,128]{2,1,0:T(8,128)(2,1)} custom-call(s32[3,16,32]{2,1,0:T(8,128)} %pad_add_fusion.table_ref, bf16[32,128,128]{2,1,0:T(8,128)(2,1)} %feat_ref.1, bf16[256,128,128]{2,1,0:T(8,128)(2,1)} %bitcast.12, f32[32,1,128]{2,1,0:T(1,128)} %bitcast.13), custom_call_target="tpu_custom_call" | custom-call | tf_op jit(solution)/shard_map/pallas_call | solution.py:255
  182.5 2.3 %copy.9 = bf16[32,128,128]{2,1,0:T(8,128)(2,1)} copy(bf16[32,128,128]{2,1,0:T(8,128)(2,1)} %shard_map.55) | data formatting | bytes 2097152
  (6 shorter events, 0.0 us)

commit v3 on v2

--- a/solution.py
+++ b/solution.py
@@ -39,7 +39,7 @@
     return places
 
 
-def scatter_kernel(nz, ny, lead, table_ref, feat_ref, weight_hbm, bias_ref, out_ref,
+def scatter_kernel(nz, ny, lead, parts, table_ref, feat_ref, weight_hbm, bias_ref, out_ref,
                    weight_ref, held, sums, staged, from_y, from_low, from_high,
                    lead_y, lead_low, lead_high,
                    weight_sem, c_send, c_recv, y_send, y_recv, up_send, up_recv, down_send, down_recv,
@@ -86,7 +86,9 @@
         def _(b):
             dst[b + start] += src[b]
 
-    rest = pl.ds(lead, owned - lead)
+    size = (owned - lead) // parts
+    starts = [lead + q * size for q in range(parts)]
+    sections = [(start, size) for start in starts] + ([(0, lead)] if lead else [])
     first = pl.ds(0, max(lead, 1))
 
     order = farthest_first(z, nz)
@@ -96,10 +98,11 @@
 
     pieces = [(h, place) for place in order for h in range(ny)]
 
-    def to_sibling(n):
+    def to_sibling(n, q):
         h, place = pieces[n]
-        return remote(staged.at[n % 2], held.at[h, place],
-                      c_send.at[h, place], c_recv.at[h, place], sibling)
+        blocks = pl.ds(*sections[q])
+        return remote(staged.at[n % 2, blocks], held.at[h, place, blocks],
+                      c_send.at[h, place, q], c_recv.at[h, place, q], sibling)
 
     def add_products(owner):
         @pl.loop(0, owned, unroll=min(8, owned))
@@ -109,16 +112,42 @@
             )
             sums[i] = product + sums[table_ref[1, owner, i]]
 
-    def to_peer(place):
-        return remote(held.at[0, place, rest], from_y.at[place], y_send.at[place], y_recv.at[place], peer)
-
-    def to_above(place):
-        return remote(held.at[ny - 1, place, rest], from_low.at[place - 1],
-                      up_send.at[place - 1], up_recv.at[place - 1], above)
-
-    def to_below(place):
-        return remote(held.at[ny - 1, place, rest], from_high.at[place],
-                      down_send.at[place], down_recv.at[place], below)
+    def went(q):
+        return pl.ds(starts[q], size)
+
+    def came(q):
+        return pl.ds(q * size, size)
+
+    def to_peer(place, q):
+        return remote(held.at[0, place, went(q)], from_y.at[place, came(q)],
+                      y_send.at[place, q], y_recv.at[place, q], peer)
+
+    def to_above(place, q):
+        return remote(held.at[ny - 1, place, went(q)], from_low.at[place - 1, came(q)],
+                      up_send.at[place - 1, q], up_recv.at[place - 1, q], above)
+
+    def to_below(place, q):
+        return remote(held.at[ny - 1, place, went(q)], from_high.at[place, came(q)],
+                      down_send.at[place, q], down_recv.at[place, q], below)
+
+    def take_y(place, q):
+        if ny > 1:
+            to_peer(place, q).wait_recv()
+            add(held.at[ny - 1, place], from_y.at[place, came(q)], starts[q])
+
+    def take_low(place, q):
+        to_above(place, q).wait_recv()
+        add(held.at[ny - 1, place], from_low.at[place - 1, came(q)], starts[q])
+
+    def take_high(place, q):
+        to_below(place, q).wait_recv()
+        add(held.at[ny - 1, place], from_high.at[place, came(q)], starts[q])
+
+    def finish(start, count):
+        @pl.loop(start, start + count)
+        def _(b):
+            total = held[ny - 1, z, b] + bias_ref[b]
+            out_ref[b] = jnp.maximum(total, 0.0).astype(out_ref.dtype)
 
     def lead_above(place):
         return remote(held.at[:, place, first], lead_low.at[place - 1],
@@ -141,23 +170,25 @@
         theirs, mine = row(place, y_of(h), 1 - c), row(place, y_of(h), c)
         add_products(theirs)
         if n >= 2:
-            to_sibling(n - 2).wait_send()
-
-        @pl.loop(0, owned)
-        def _(b):
-            staged[n % 2, b] = sums[table_ref[2, theirs, b]]
-
-        to_sibling(n).start()
+            for q in range(len(sections)):
+                to_sibling(n - 2, q).wait_send()
+        for q, (start, count) in enumerate(sections):
+            @pl.loop(start, start + count)
+            def _(b):
+                staged[n % 2, b] = sums[table_ref[2, theirs, b]]
+
+            to_sibling(n, q).start()
         add_products(mine)
-        to_sibling(n).wait_recv()
-
-        @pl.loop(0, owned)
-        def _(b):
-            held[h, place, b] += sums[table_ref[2, mine, b]]
-
-        if h < ny - 1:
-            to_peer(place).start()
-        elif lead:
+        for q, (start, count) in enumerate(sections):
+            to_sibling(n, q).wait_recv()
+
+            @pl.loop(start, start + count)
+            def _(b):
+                held[h, place, b] += sums[table_ref[2, mine, b]]
+
+            if h < ny - 1 and q < parts:
+                to_peer(place, q).start()
+        if h == ny - 1 and lead:
             pl.when((place > z) & (z == 0))(lambda: lead_above(place).start())
             pl.when((place < z) & (z == nz - 1))(lambda: lead_below(place).start())
 
@@ -176,25 +207,18 @@
                 lead_below(place).start()
 
     for t, place in enumerate(order[:-1]):
-        if ny > 1:
-            to_peer(place).wait_recv()
-            add(held.at[ny - 1, place], from_y.at[place], lead)
-
-        @pl.when(place > z)
-        def _():
-            @pl.when(has_below)
-            def _():
-                to_above(place).wait_recv()
-                add(held.at[ny - 1, place], from_low.at[place - 1], lead)
-            to_above(place).start()
-
-        @pl.when(place < z)
-        def _():
-            @pl.when(has_above)
-            def _():
-                to_below(place).wait_recv()
-                add(held.at[ny - 1, place], from_high.at[place], lead)
-            to_below(place).start()
+        for q in range(parts):
+            take_y(place, q)
+
+            @pl.when(place > z)
+            def _():
+                pl.when(has_below)(lambda: take_low(place, q))
+                to_above(place, q).start()
+
+            @pl.when(place < z)
+            def _():
+                pl.when(has_above)(lambda: take_high(place, q))
+                to_below(place, q).start()
 
         if lead and t == 1:
             @pl.when(has_below)
@@ -208,38 +232,28 @@
                 add_lead(z, lead_high.at[z])
             lead_peer().start()
 
-    if ny > 1:
-        to_peer(z).wait_recv()
-        add(held.at[ny - 1, z], from_y.at[z], lead)
+    for q in range(parts):
+        take_y(z, q)
+        pl.when(has_below)(lambda: take_low(z, q))
+        pl.when(has_above)(lambda: take_high(z, q))
+        finish(starts[q], size)
     if lead:
         lead_peer().wait_recv()
         add(held.at[ny - 1, z], lead_y)
-
-    @pl.when(has_below)
-    def _():
-        to_above(z).wait_recv()
-        add(held.at[ny - 1, z], from_low.at[z - 1], lead)
-
-    @pl.when(has_above)
-    def _():
-        to_below(z).wait_recv()
-        add(held.at[ny - 1, z], from_high.at[z], lead)
-
-    @pl.loop(0, owned)
-    def _(b):
-        total = held[ny - 1, z, b] + bias_ref[b]
-        out_ref[b] = jnp.maximum(total, 0.0).astype(out_ref.dtype)
+        finish(0, lead)
 
     for n in range(max(0, len(pieces) - 2), len(pieces)):
-        to_sibling(n).wait_send()
+        for q in range(len(sections)):
+            to_sibling(n, q).wait_send()
     for place in order:
-        if ny > 1:
-            to_peer(place).wait_send()
-        pl.when(place > z)(lambda place=place: to_above(place).wait_send())
-        pl.when(place < z)(lambda place=place: to_below(place).wait_send())
+        for q in range(parts):
+            if ny > 1:
+                to_peer(place, q).wait_send()
+            pl.when(place > z)(lambda: to_above(place, q).wait_send())
+            pl.when(place < z)(lambda: to_below(place, q).wait_send())
         if lead:
-            pl.when(place > z)(lambda place=place: lead_above(place).wait_send())
-            pl.when(place < z)(lambda place=place: lead_below(place).wait_send())
+            pl.when(place > z)(lambda: lead_above(place).wait_send())
+            pl.when(place < z)(lambda: lead_below(place).wait_send())
     if lead:
         lead_peer().wait_send()
 
@@ -248,12 +262,13 @@
     owned, samples, width = features.shape
     chunk = (owned, samples, width)
     lead = owned * 5 // 32 if ny > 1 and nz > 2 else 0
+    parts = next((p for p in (3, 2) if ny > 1 and (owned - lead) % p == 0), 1)
     rest = (owned - lead,) + chunk[1:]
     first = (max(lead, 1),) + chunk[1:]
     dma = pltpu.SemaphoreType.DMA
     vmem = pl.BlockSpec(memory_space=pltpu.VMEM)
     return pl.pallas_call(
-        functools.partial(scatter_kernel, nz, ny, lead),
+        functools.partial(scatter_kernel, nz, ny, lead, parts),
         out_shape=jax.ShapeDtypeStruct(chunk, jnp.bfloat16),
         in_specs=[pl.BlockSpec(memory_space=pltpu.SMEM), vmem, pl.BlockSpec(memory_space=pl.ANY), vmem],
         out_specs=vmem,
@@ -269,10 +284,10 @@
             pltpu.VMEM((nz - 1, ny) + first if lead else (1, 1) + first, jnp.float32),
             pltpu.VMEM((nz - 1, ny) + first if lead else (1, 1) + first, jnp.float32),
             dma,
-            dma((ny, nz)), dma((ny, nz)),
-            dma((nz,)), dma((nz,)),
-            dma((nz,)), dma((nz,)),
-            dma((nz,)), dma((nz,)),
+            dma((ny, nz, parts + 1)), dma((ny, nz, parts + 1)),
+            dma((nz, parts)), dma((nz, parts)),
+            dma((nz, parts)), dma((nz, parts)),
+            dma((nz, parts)), dma((nz, parts)),
             dma, dma,
             dma((nz,)), dma((nz,)),
             dma((nz,)), dma((nz,)),

time: 185 us -> 183 us (0.989)
  Pallas kernels: 180 us -> 178 us
    pallas_call x1, Pallas kernels: 180 us -> 178 us  [scatter_sum(): pl.pallas_call(functools.partial(scatter_kernel, nz, ny, lead, parts), ou...]
where the time goes in v3:
time: 183 us
  Pallas kernels  178 us (97%)
  local copies, waits for them, and re-layouts  3.09 us (2%)
    pallas_call x1, Pallas kernels, scatter_sum(): pl.pallas_call(functools.partial(scatter_kernel, nz, ny, lead, parts), ou...  178 us

profile of v3, /device:TPU:0, one launch (start us, length us, event | category | flops | bytes accessed | tf_op | source)
XLA Modules:
  0.0 182.5 jit_solution(13384699014300113645)
XLA Ops:
  0.0 0.8 dynamic-slice_bitcast_fusion
  0.8 0.1 select_reduce_fusion.3
  0.9 0.7 select_reduce_fusion.1
  1.6 0.6 pad_add_fusion.table_ref
  2.3 177.9 %shard_map.55 = bf16[32,128,128]{2,1,0:T(8,128)(2,1)} custom-call(s32[3,16,32]{2,1,0:T(8,128)} %pad_add_fusion.table_ref, bf16[32,128,128]{2,1,0:T(8,128)(2,1)} %feat_ref.1, bf16[256,128,128]{2,1,0:T(8,128)(2,1)} %bitcast.12, f32[32,1,128]{2,1,0:T(1,128)} %bitcast.13), custom_call_target="tpu_custom_call" | custom-call | tf_op jit(solution)/shard_map/pallas_call | solution.py:270
  180.2 2.3 %copy.9 = bf16[32,128,128]{2,1,0:T(8,128)(2,1)} copy(bf16[32,128,128]{2,1,0:T(8,128)(2,1)} %shard_map.55) | data formatting | bytes 2097152
  (6 shorter events, 0.0 us)
